TPU v7x, 32 devices: a whole 2x2x4 slice. The times are simulated.
32 devices in a mesh: gx: 4 (over z), gy: 4 (over y, x), layer: 2 (over core).
Axes of the slice: x: 2, y: 2, z: 4, core: 2. Of those that a mesh axis runs over, the one named last changes fastest.
Arguments:
- load_current: float32 [8, 64, 2048], P('layer', 'gx', 'gy'), may hold values from -12 to 12
- pad_cond: float32 [8, 64, 2048], P('layer', 'gx', 'gy'), may hold values from 0.01 to 0.1
- cond_x: float32 [8, 64, 2048], P('layer', 'gx', 'gy'), may hold values from 0.5 to 4
- cond_y: float32 [8, 64, 2048], P('layer', 'gx', 'gy'), may hold values from 0.5 to 4
- via_map: int32 [8, 64, 2048], P('layer', 'gx', 'gy'), may hold values from 0 to 3
- branch_index: int32 [4096, 256], P(('gx', 'gy', 'layer')), may hold values from 0 to 7679
- tree_owner: int32 [4096, 1], P(('gx', 'gy', 'layer')), may hold values from 0 to 15; in each aligned block of 128 rows (0 to 127, 128 to 255, ...) at most 16 rows name the same one
- initial_stress: float32 [4096, 256], P(('gx', 'gy', 'layer')), may hold values from -6 to 6
- block_inverse: float32 [16, 256, 256], P(('gx', 'gy')), may hold values from -1.5 to 1.5
Outputs:
- drop: float32 [8, 64, 2048], P('layer', 'gx', 'gy')
- final_stress: float32 [4096, 256], P(('gx', 'gy', 'layer'))
Inputs may be any that keep to these rules, and one draw needn't show every extreme that they name: `tree_owner`: among the 128 trees of one device at most 16 have one owner, and some owner has exactly 16. Owners count in gx+gy order within the tree's own layer group. `branch_index`: A branch joins a node to its next node along x inside the home tile.
All inputs are finite; a program needn't handle non-finite values.
Results may differ from a plain program's by a relative error of at most 0.0003.
Values sent between devices are 32-bit elements; how exact they have to be, the bound alone decides.
A program may use at most 64 MiB of HBM per device.

v0:
```python
import jax
import jax.numpy as jnp
from jax import lax
from jax.sharding import PartitionSpec as P

KX = 2
KY = 4
ITERS = 2
SWEEPS = 4
STEPS = 8


OMEGA = 0.7
TAU = 0.6
VIA_G = 1.5
COARSE_G = 64.0
KAPPA = 2.0


def padded_2(block, sides, width):
    for axis, dim in sides:
        count = lax.axis_size(axis)
        forward = [(i, i + 1) for i in range(count - 1)]
        backward = [(target, source) for source, target in forward]
        low = lax.ppermute(
            lax.slice_in_dim(block, block.shape[dim] - width, None, axis=dim), axis, forward
        )
        high = lax.ppermute(lax.slice_in_dim(block, 0, width, axis=dim), axis, backward)
        block = jnp.concatenate([low, block, high], axis=dim)
    return block


def grid_rims(stacked):
    return padded_2(stacked, (("gx", 2), ("gy", 3), ("layer", 1)), 1)


def total(values):
    return lax.psum(values, ("gx", "gy", "layer"))


def per_device(
    load_current,
    pad_cond,
    cond_x,
    cond_y,
    via_map,
    branch_index,
    tree_owner,
    initial_stress,
    block_inverse,
):
    layers, rows, cols = load_current.shape
    size_x = lax.axis_size("gx")
    size_y = lax.axis_size("gy")
    size_l = lax.axis_size("layer")
    glob_i = lax.axis_index("gx") * rows + jnp.arange(rows, dtype=jnp.int32)
    glob_j = lax.axis_index("gy") * cols + jnp.arange(cols, dtype=jnp.int32)
    glob_l = lax.axis_index("layer") * layers + jnp.arange(layers, dtype=jnp.int32)
    mask_x = (glob_i < rows * size_x - 1).astype(jnp.float32)
    mask_y = (glob_j < cols * size_y - 1).astype(jnp.float32)
    mask_z = (glob_l < layers * size_l - 1).astype(jnp.float32)
    link_x = cond_x * mask_x[None, :, None]
    link_y = cond_y * mask_y[None, None, :]
    link_z = via_map.astype(jnp.float32) * VIA_G * mask_z[:, None, None]
    links = grid_rims(jnp.stack([link_x, link_y, link_z]))
    down_x = links[0, 1:-1, :-2, 1:-1]
    down_y = links[1, 1:-1, 1:-1, :-2]
    down_z = links[2, :-2, 1:-1, 1:-1]
    diag = pad_cond + link_x + down_x + link_y + down_y + link_z + down_z

    def restrict(field):
        return jnp.sum(field.reshape(layers, KX, rows // KX, KY, cols // KY), axis=(0, 2, 4))

    def prolong(coarse):
        spread = jnp.broadcast_to(
            coarse[None, :, None, :, None], (layers, KX, rows // KX, KY, cols // KY)
        )
        return spread.reshape(layers, rows, cols)

    cdiag_own = restrict(pad_cond)

    def collect(small):
        every = lax.all_gather(small.reshape(1, KX * KY), ("gx", "gy", "layer"), axis=0, tiled=True)
        shaped = every.reshape(size_x, size_y, size_l, KX, KY).transpose(2, 0, 3, 1, 4)
        return shaped.reshape(size_l, size_x * KX, size_y * KY)

    cdiag_all = collect(cdiag_own)
    cdiag_full = cdiag_all + 6.0 * COARSE_G

    def coarse_solve(coarse_rhs):
        rhs_all = collect(coarse_rhs)
        value = jnp.zeros_like(rhs_all)
        for sweep in range(SWEEPS):
            padded = jnp.pad(value, 1)
            beside_all = padded[:-2, 1:-1, 1:-1] + padded[2:, 1:-1, 1:-1]
            beside_all = beside_all + padded[1:-1, 2:, 1:-1] + padded[1:-1, :-2, 1:-1]
            beside_all = beside_all + padded[1:-1, 1:-1, 2:] + padded[1:-1, 1:-1, :-2]
            value = (
                value + TAU * (rhs_all - (cdiag_full * value - COARSE_G * beside_all)) / cdiag_full
            )
        start = (lax.axis_index("layer"), lax.axis_index("gx") * KX, lax.axis_index("gy") * KY)
        return lax.dynamic_slice(value, start, (1, KX, KY))[0]

    def precondition(resid):
        return OMEGA * resid / diag + prolong(coarse_solve(restrict(resid)))

    drop = jnp.zeros_like(load_current)
    resid = load_current
    zvec = precondition(resid)
    direction = zvec
    rz_now = total(jnp.sum(resid * zvec))
    for step in range(ITERS):
        operate_padded = grid_rims(direction[None])[0]
        out = pad_cond * direction
        out = (
            out
            + link_x * (direction - operate_padded[1:-1, 2:, 1:-1])
            + down_x * (direction - operate_padded[1:-1, :-2, 1:-1])
        )
        out = (
            out
            + link_y * (direction - operate_padded[1:-1, 1:-1, 2:])
            + down_y * (direction - operate_padded[1:-1, 1:-1, :-2])
        )
        out = (
            out
            + link_z * (direction - operate_padded[2:, 1:-1, 1:-1])
            + down_z * (direction - operate_padded[:-2, 1:-1, 1:-1])
        )
        alpha = rz_now / total(jnp.sum(direction * out))
        drop = drop + alpha * direction
        resid = resid - alpha * out
        if step + 1 < ITERS:
            zvec = precondition(resid)
            rz_next = total(jnp.sum(resid * zvec))
            direction = zvec + rz_next / rz_now * direction
            rz_now = rz_next
    trees_dev, segs = initial_stress.shape
    owners_count = size_x * size_y
    capacity = 2 * trees_dev // owners_count
    seg_layer = (jnp.arange(segs, dtype=jnp.int32) % layers)[None, :]
    cell = seg_layer * (rows * cols) + branch_index
    flat_drop = drop.reshape(-1)
    flat_link = link_x.reshape(-1)
    current = flat_link[cell] * (flat_drop[cell] - flat_drop[cell + cols])
    owners = tree_owner[:, 0]
    hits = (owners[:, None] == jnp.arange(owners_count, dtype=jnp.int32)[None, :]).astype(jnp.int32)
    slot_rank = jnp.sum((jnp.cumsum(hits, axis=0) - hits) * hits, axis=1)
    payload = jnp.stack([current, initial_stress])
    outgoing = (
        jnp.zeros((2, owners_count, capacity, segs), jnp.float32)
        .at[:, owners, slot_rank]
        .set(payload)
    )
    inverse = block_inverse[0]
    piece = lax.all_to_all(outgoing, ("gx", "gy"), split_axis=1, concat_axis=1, tiled=True)
    count = piece.shape[2]
    flow = piece[0].reshape(-1, segs)
    stress = piece[1].reshape(-1, segs)
    for step in range(STEPS):
        stress = jnp.einsum(
            "ts,us->tu", stress + KAPPA * flow, inverse, precision=lax.Precision.HIGHEST
        )
    returning = stress.reshape(owners_count, count, segs)
    solved = lax.all_to_all(returning, ("gx", "gy"), split_axis=0, concat_axis=0, tiled=True)
    final_stress = solved[owners, slot_rank]
    return (drop, final_stress)


def solution(mesh):
    return jax.shard_map(
        per_device,
        mesh=mesh,
        in_specs=(
            P("layer", "gx", "gy"),
            P("layer", "gx", "gy"),
            P("layer", "gx", "gy"),
            P("layer", "gx", "gy"),
            P("layer", "gx", "gy"),
            P(("gx", "gy", "layer"), None),
            P(("gx", "gy", "layer"), None),
            P(("gx", "gy", "layer"), None),
            P(("gx", "gy"), None, None),
        ),
        out_specs=(P("layer", "gx", "gy"), P(("gx", "gy", "layer"), None)),
        check_vma=False,
    )
```

profile of v0, /device:TPU:0, one launch (start us, length us, event | category | flops | bytes accessed | tf_op | source)
XLA Modules:
  0.0 902.8 jit_solution(7220110713637692259)
XLA Ops:
  1.9 4.9 collective-permute-start
  8.4 42.6 %all-gather.1 = f32[32,1,8]{2,1,0:T(1,128)S(1)} all-gather(f32[1,1,8]{2,1,0:T(1,128)S(1)} %reshape.172), channel_id=1, replica_groups=mesh['gx'=4,'gy'=4,'layer'=2] {'gx','gy','layer'}, dimensions={0}, use_global_device_ids=true | all-gather | bytes 1056 | tf_op jit(solution)/shard_map/all_gather | solution.py:83
  51.5 36.4 %all-gather = f32[32,1,8]{2,1,0:T(1,128)S(1)} all-gather(f32[1,1,8]{2,1,0:T(1,128)S(1)} %reshape.170), channel_id=1, replica_groups=mesh['gx'=4,'gy'=4,'layer'=2] {'gx','gy','layer'}, dimensions={0}, use_global_device_ids=true | all-gather | bytes 1056 | tf_op jit(solution)/shard_map/all_gather | solution.py:83
  90.3 3.6 collective-permute-start.2
  95.3 2.2 collective-permute-done.2
  97.5 4.1 collective-permute-done.3
  107.0 4.1 collective-permute-done.6
  111.2 3.2 collective-permute-start.7
  116.2 4.3 collective-permute-done.8
  121.9 3.0 collective-permute-start.9
  126.9 39.2 %all-reduce.7 = (f32[]{:T(128)}, f32[]{:T(128)}) all-reduce(f32[]{:T(128)} %get-tuple-element.3, f32[]{:T(128)} %get-tuple-element.2), channel_id=1, replica_groups=mesh['gx'=4,'gy'=4,'layer'=2] {'gx','gy','layer'}, use_global_device_ids=true, to_apply=%region_5.6 | all-reduce | flops 2 | bytes 16 | tf_op jit(solution)/shard_map/psum | solution.py:38
  167.6 41.0 %all-gather.2 = f32[32,1,8]{2,1,0:T(1,128)S(1)} all-gather(f32[1,1,8]{2,1,0:T(1,128)S(1)} %reshape.174), channel_id=1, replica_groups=mesh['gx'=4,'gy'=4,'layer'=2] {'gx','gy','layer'}, dimensions={0}, use_global_device_ids=true | all-gather | bytes 1056 | tf_op jit(solution)/shard_map/all_gather | solution.py:83
  210.7 37.1 %psum.30 = f32[]{:T(128)} all-reduce(f32[]{:T(128)} %get-tuple-element.8), channel_id=1, replica_groups=mesh['gx'=4,'gy'=4,'layer'=2] {'gx','gy','layer'}, use_global_device_ids=true, to_apply=%region_11.12 | all-reduce | flops 1 | bytes 8 | tf_op jit(solution)/shard_map/psum | solution.py:38
  249.0 4.8 collective-permute-start.11
  255.4 4.0 collective-permute-done.12
  259.4 4.2 collective-permute-start.13
  265.4 4.3 collective-permute-done.14
  275.2 180.5 %gather_fusion = f32[32768]{0:T(1024)S(1)} fusion(f32[32768]{0:T(1024)S(1)} %bitcast.94, s32[32768]{0:T(1024)S(1)} %broadcast_clamp_fusion.1), kind=kCustom, calls=%fused_computation | custom fusion | bytes 393216 | tf_op jit(solution)/shard_map/gather | solution.py:145
  455.8 39.4 %psum.31 = f32[]{:T(128)} all-reduce(f32[]{:T(128)} %fusion.22), channel_id=1, replica_groups=mesh['gx'=4,'gy'=4,'layer'=2] {'gx','gy','layer'}, use_global_device_ids=true, to_apply=%region_13.14 | all-reduce | flops 1 | bytes 8 | tf_op jit(solution)/shard_map/psum | solution.py:38
  497.2 180.5 %gather_fusion.1 = f32[32768]{0:T(1024)S(1)} fusion(f32[32768]{0:T(1024)S(1)} %bitcast.92, s32[32768]{0:T(1024)S(1)} %broadcast_clamp_fusion.1), kind=kCustom, calls=%fused_computation.1 | custom fusion | bytes 393216 | tf_op jit(solution)/shard_map/gather | solution.py:145
  677.7 180.5 %gather_fusion.2 = f32[32768]{0:T(1024)S(1)} fusion(f32[32768]{0:T(1024)S(1)} %bitcast.93, s32[32768]{0:T(1024)S(1)} %broadcast_clamp_fusion), kind=kCustom, calls=%fused_computation.2 | custom fusion | bytes 393216 | tf_op jit(solution)/shard_map/gather | solution.py:145
  859.6 5.7 scatter_fusion
  865.4 19.4 %all_to_all.10 = f32[2,16,16,256]{3,0,2,1:T(2,128)S(1)} all-to-all(f32[2,16,16,256]{3,0,2,1:T(2,128)S(1)} %scatter_fusion), channel_id=1, replica_groups=mesh['gx'=4,'gy'=4,'layer'=2] {'gx','gy'}, dimensions={1} | all-to-all | bytes 1048576 | tf_op jit(solution)/shard_map/all_to_all | solution.py:156
  888.7 12.1 %all_to_all.11 = f32[16,16,256]{2,1,0:T(8,128)S(1)} all-to-all(f32[16,16,256]{2,1,0:T(8,128)S(1)} %fusion), channel_id=1, replica_groups=mesh['gx'=4,'gy'=4,'layer'=2] {'gx','gy'}, dimensions={0} | all-to-all | bytes 524288 | tf_op jit(solution)/shard_map/all_to_all | solution.py:165
  (129 shorter events, 36.5 us)
Async XLA Ops:
  0.6 884.7 %copy-start = (f32[1,256,256]{2,1,0:T(8,128)S(1)}, f32[1,256,256]{2,1,0:T(8,128)}, u32[]{:S(2)}) copy-start(f32[1,256,256]{2,1,0:T(8,128)} %param.17) | copy-start | bytes 786436
  0.7 1.1 copy-start.4
  0.7 1.1 copy-start.5
  1.9 6.3 copy-start.3
  1.9 88.2 %collective-permute-start = (f32[3,4,1,512]{3,2,1,0:T(1,128)S(1)}, f32[3,4,1,512]{3,2,1,0:T(1,128)S(1)}, u32[]{:S(2)}, u32[]{:S(2)}) collective-permute-start(f32[3,4,1,512]{3,2,1,0:T(1,128)S(1)} %get-tuple-element.23), channel_id=1, source_target_pairs={{0,8},{8,16},{16,24},{1,9},{9,17},{17,25},{2,10},{10,18},{18,26},{... | collective-permute-start | bytes 73736 | tf_op jit(solution)/shard_map/ppermute | solution.py:25
  6.9 83.3 %collective-permute-start.1 = (f32[3,4,1,512]{3,2,1,0:T(1,128)S(1)}, f32[3,4,1,512]{3,2,1,0:T(1,128)S(1)}, u32[]{:S(2)}, u32[]{:S(2)}) collective-permute-start(f32[3,4,1,512]{3,2,1,0:T(1,128)S(1)} %get-tuple-element.22), channel_id=1, source_target_pairs={{8,0},{16,8},{24,16},{9,1},{17,9},{25,17},{10,2},{18,10},{26,18},{... | collective-permute-start | bytes 73736 | tf_op jit(solution)/shard_map/ppermute | solution.py:28
  8.2 43.1 %copy-start.2 = (f32[4,16,512]{2,1,0:T(8,128)S(1)}, f32[4,16,512]{2,1,0:T(8,128)}, u32[]{:S(2)}) copy-start(f32[4,16,512]{2,1,0:T(8,128)} %param.9) | copy-start | bytes 393220
  90.3 7.2 collective-permute-start.2
  93.9 7.7 collective-permute-start.3
  101.8 2.3 collective-permute-start.4
  103.1 1.0 copy-start.1
  104.3 2.7 collective-permute-start.5
  105.6 5.6 collective-permute-start.6
  111.2 4.9 collective-permute-start.7
  114.5 6.0 collective-permute-start.8
  120.6 4.4 collective-permute-start.10
  121.9 3.9 collective-permute-start.9
  249.0 6.4 collective-permute-start.11
  253.8 1.3 copy-start.9
  253.8 5.5 collective-permute-start.12
  259.4 5.9 collective-permute-start.13
  263.6 6.0 collective-permute-start.14
  269.7 2.7 collective-permute-start.15
  271.0 3.1 collective-permute-start.16
  (3 other events, 2.5 us)
where the time goes:
time: 904 us; the launch traced here: 903 us
  local copies, waits for them, and re-layouts  553 us (61%)
  blocking collectives  267 us (30%)
  starting transfers between devices  38 us (4%)
  waiting for transfers between devices  27 us (3%)
    gather x3, local copies, waits for them, and re-layouts, per_device(): current = flat_link[cell] * (flat_drop[cell] - flat_drop[cell + cols])  542 us
    all_gather x3, blocking collectives, collect(): lax.all_gather(small.reshape(1, KX * KY), ('gx', 'gy', 'layer'), axis=0,...  120 us
    psum x3, blocking collectives, total(): return lax.psum(values, ('gx', 'gy', 'layer'))  116 us
    ppermute x9, starting transfers between devices, padded_2(): lax.ppermute(lax.slice_in_dim(block, block.shape[dim] - width, None, axis...  27.6 us
    ppermute x8, waiting for transfers between devices, padded_2(): lax.ppermute(lax.slice_in_dim(block, 0, width, axis=dim), axis, backward)  22.5 us
    all_to_all x1, blocking collectives, per_device(): lax.all_to_all(outgoing, ('gx', 'gy'), split_axis=1, concat_axis=1, tiled...  19.4 us
  transfers between devices with their start and end apart: 17, of which 11 were waited for; matrix products, arithmetic and copies ran while one was open for 0% of the time, Pallas kernels for 0%

commit v1 on v0

v1 whole, which is shorter than its diff:
```python
import functools

import jax
import jax.numpy as jnp
from jax import lax
from jax.experimental import pallas as pl
from jax.experimental.pallas import tpu as pltpu
from jax.sharding import PartitionSpec as P

KX = 2
KY = 4
SWEEPS = 4
STEPS = 8

OMEGA = 0.7
TAU = 0.6
VIA_G = 1.5
COARSE_G = 64.0
KAPPA = 2.0
LANES = 128
HALF = 64
MESH = pl.DeviceIdType.MESH


def iota(shape, dim):
    return lax.broadcasted_iota(jnp.int32, shape, dim)


def sum_all(v):
    while v.ndim > 2:
        v = jnp.sum(v, axis=0)
    return jnp.sum(jnp.sum(v, axis=0, keepdims=True), axis=1, keepdims=True)


def cg_kernel(
    sizes,
    load_ref, pad_ref, cx_ref, cy_ref, via_ref,
    drop_ref, flow_ref,
    links, downs, dinv_ref, w_ref, p_ref, q_ref,
    xsend, xrecv, yrecv, zrecv, lxsend, lxrecv, lyrecv, lzrecv,
    tsend, trecv,
    link_send, link_recv, halo_send, halo_recv, tile_send, tile_recv,
):
    sx, sy, sl = sizes
    n = sx * sy * sl
    layers, rows, cols = load_ref.shape
    br, bc = rows // KX, cols // KY
    nyc = KY * sy
    grid_rows = KX * sx
    gx, gy, gl = lax.axis_index("gx"), lax.axis_index("gy"), lax.axis_index("layer")
    me = (gx * sy + gy) * sl + gl

    def coords(flat):
        return (flat // (sy * sl), (flat // sl) % sy, flat % sl)

    barrier = pltpu.get_barrier_semaphore()

    def greet(k, carry):
        pl.semaphore_signal(
            barrier, inc=1, device_id=coords(lax.rem(me + k, n)), device_id_type=MESH
        )
        return carry

    lax.fori_loop(1, n, greet, 0)

    up_dev = (
        (lax.rem(gx + 1, sx), gy, gl),
        (gx, lax.rem(gy + 1, sy), gl),
        (gx, gy, lax.rem(gl + 1, sl)),
    )
    down_dev = (
        (lax.rem(gx + sx - 1, sx), gy, gl),
        (gx, lax.rem(gy + sy - 1, sy), gl),
        (gx, gy, lax.rem(gl + sl - 1, sl)),
    )

    shape = (layers, rows, cols)
    plane_of = iota(shape, 0)
    row_of = iota(shape, 1)
    col_of = iota(shape, 2)
    links[0] = jnp.where(gx * rows + row_of < rows * sx - 1, cx_ref[...], 0.0)
    links[1] = jnp.where(gy * cols + col_of < cols * sy - 1, cy_ref[...], 0.0)
    links[2] = jnp.where(
        gl * layers + plane_of < layers * sl - 1, via_ref[...].astype(jnp.float32) * VIA_G, 0.0
    )
    lxsend[...] = links[0, :, rows - 1 : rows, :]

    tile_shape = (grid_rows, LANES)
    trow = iota(tile_shape, 0)
    tlane = iota(tile_shape, 1)
    lane0 = gl * nyc + gy * KY
    valid = tlane < sl * nyc

    def restrict_into(tile, field, shift):
        flat = jnp.sum(field, axis=0)
        for a in range(KX):
            for b in range(KY):
                val = sum_all(flat[a * br : (a + 1) * br, b * bc : (b + 1) * bc])
                here = (trow == gx * KX + a) & (tlane == lane0 + b + shift)
                tile = jnp.where(here, val, tile)
        return tile

    def send_tile(phase):
        def one(k, carry):
            pltpu.make_async_remote_copy(
                src_ref=tsend.at[phase],
                dst_ref=trecv.at[phase, k - 1],
                send_sem=tile_send.at[phase],
                recv_sem=tile_recv.at[phase],
                device_id=coords(lax.rem(me + k, n)),
                device_id_type=MESH,
            ).start()
            return carry

        lax.fori_loop(1, n, one, 0)

    def wait_tile(phase):
        every = trecv.at[phase]
        pltpu.make_async_copy(every, every, tile_recv.at[phase]).wait()
        return jnp.sum(trecv[phase], axis=0) + tsend[phase]

    def drain_tile(phase):
        every = trecv.at[phase]
        pltpu.make_async_copy(every, every, tile_send.at[phase]).wait()

    tile = jnp.zeros(tile_shape, jnp.float32)
    tile = restrict_into(tile, load_ref[...], 0)
    tsend[0] = restrict_into(tile, pad_ref[...], HALF)

    def remote(src, dst, send, recv, device):
        return pltpu.make_async_remote_copy(
            src_ref=src, dst_ref=dst, send_sem=send, recv_sem=recv,
            device_id=device, device_id_type=MESH,
        )

    last = pl.ds(cols - LANES, LANES)
    link_copies = [
        remote(lxsend, lxrecv, link_send.at[0], link_recv.at[0], up_dev[0]),
        remote(links.at[1, :, :, last], lyrecv, link_send.at[1], link_recv.at[1], up_dev[1]),
        remote(links.at[2, layers - 1], lzrecv, link_send.at[2], link_recv.at[2], up_dev[2]),
    ]

    def halo_copies(h):
        pairs = [
            (xsend.at[h, 0], xrecv.at[h, 0], up_dev[0]),
            (xsend.at[h, 1], xrecv.at[h, 1], down_dev[0]),
            (w_ref.at[h, :, :, last], yrecv.at[h, 0], up_dev[1]),
            (w_ref.at[h, :, :, pl.ds(0, LANES)], yrecv.at[h, 1], down_dev[1]),
            (w_ref.at[h, layers - 1], zrecv.at[h, 0], up_dev[2]),
            (w_ref.at[h, 0], zrecv.at[h, 1], down_dev[2]),
        ]
        return [
            remote(src, dst, halo_send.at[h, i], halo_recv.at[h, i], dev)
            for i, (src, dst, dev) in enumerate(pairs)
        ]

    def from_below(v, x_lo, y_lo, z_lo):
        vx = jnp.where(row_of == 0, x_lo, pltpu.roll(v, 1, 1))
        edge = jnp.concatenate([pltpu.roll(y_lo, 1, 2), v[:, :, LANES:]], axis=2)
        vy = jnp.where(col_of == 0, edge, pltpu.roll(v, 1, 2))
        vz = jnp.concatenate([z_lo[None], v[:-1]], axis=0)
        return vx, vy, vz

    def from_above(v, x_hi, y_hi, z_hi):
        vx = jnp.where(row_of == rows - 1, x_hi, pltpu.roll(v, rows - 1, 1))
        edge = jnp.concatenate([v[:, :, :-LANES], pltpu.roll(y_hi, LANES - 1, 2)], axis=2)
        vy = jnp.where(col_of == cols - 1, edge, pltpu.roll(v, cols - 1, 2))
        vz = jnp.concatenate([v[1:], z_hi[None]], axis=0)
        return vx, vy, vz

    pl.semaphore_wait(barrier, n - 1)
    for copy in link_copies:
        copy.start()
    send_tile(0)

    for copy in link_copies:
        copy.wait()
    down_x, _, _ = from_below(links[0], lxrecv[...], lyrecv[...], lzrecv[...])
    _, down_y, _ = from_below(links[1], lxrecv[...], lyrecv[...], lzrecv[...])
    _, _, down_z = from_below(links[2], lxrecv[...], lyrecv[...], lzrecv[...])
    downs[0] = down_x
    downs[1] = down_y
    downs[2] = down_z
    diag = pad_ref[...] + links[0] + down_x + links[1] + down_y + links[2] + down_z
    dinv = OMEGA / diag
    dinv_ref[...] = dinv
    w0 = load_ref[...] * dinv

    def put_halo(h, w):
        w_ref[h] = w
        xsend[h, 0] = w[:, rows - 1 : rows, :]
        xsend[h, 1] = w[:, 0:1, :]

    put_halo(0, w0)
    first = halo_copies(0)
    for copy in first:
        copy.start()

    total0 = wait_tile(0)
    c0 = jnp.where(valid, total0, 0.0)
    cfull = jnp.where(valid, pltpu.roll(total0, LANES - HALF, 1), 0.0) + 6.0 * COARSE_G
    in_layer = lax.rem(tlane, nyc)

    def coarse(c):
        y = TAU * c / cfull
        for _ in range(SWEEPS - 1):
            near = jnp.where(trow > 0, pltpu.roll(y, 1, 0), 0.0)
            near += jnp.where(trow < grid_rows - 1, pltpu.roll(y, grid_rows - 1, 0), 0.0)
            near += jnp.where(in_layer > 0, pltpu.roll(y, 1, 1), 0.0)
            near += jnp.where(in_layer < nyc - 1, pltpu.roll(y, LANES - 1, 1), 0.0)
            near += jnp.where(tlane >= nyc, pltpu.roll(y, nyc, 1), 0.0)
            near += jnp.where(tlane < (sl - 1) * nyc, pltpu.roll(y, LANES - nyc, 1), 0.0)
            y = y + TAU * (c - (cfull * y - COARSE_G * near)) / cfull
            y = jnp.where(valid, y, 0.0)
        return y

    def spread(y):
        t = pltpu.roll(y, lax.rem(grid_rows + 1 - gx * KX, grid_rows), 0)
        t = pltpu.roll(t, lax.rem(LANES + 1 - lane0, LANES), 1)

        def bcast(src, r, c, height):
            return jnp.broadcast_to(src[r : r + 1, c : c + 1], (height, bc))

        def across(src, r, height):
            return jnp.concatenate([bcast(src, r, 1 + b, height) for b in range(KY)], axis=1)

        def whole(src):
            return jnp.concatenate([across(src, 1 + a, br) for a in range(KX)], axis=0)

        def side(c):
            parts = [
                jnp.broadcast_to(t[1 + a : 2 + a, c : c + 1], (br, LANES)) for a in range(KX)
            ]
            return jnp.concatenate(parts, axis=0)

        above = pltpu.roll(t, LANES - nyc, 1)
        below = pltpu.roll(t, nyc, 1)
        return (
            whole(t),
            (across(t, 0, 1), across(t, KX + 1, 1)),
            (side(0), side(KY + 1)),
            (whole(below), whole(above)),
        )

    def operate(v, lows, highs):
        bx, by, bz = from_below(v, *lows)
        ax, ay, az = from_above(v, *highs)
        out = pad_ref[...] * v
        out = out + links[0] * (v - ax) + downs[0] * (v - bx)
        out = out + links[1] * (v - ay) + downs[1] * (v - by)
        return out + links[2] * (v - az) + downs[2] * (v - bz)

    y0 = coarse(c0)
    own0, x0, yy0, z0 = spread(y0)
    coarse_dot0 = sum_all(c0 * y0)
    p0 = w0 + own0[None]
    p_ref[...] = p0
    for copy in first:
        copy.wait()

    lows0 = (xrecv[0, 0] + x0[0][None], yrecv[0, 0] + yy0[0][None], zrecv[0, 0] + z0[0])
    highs0 = (xrecv[0, 1] + x0[1][None], yrecv[0, 1] + yy0[1][None], zrecv[0, 1] + z0[1])
    q0 = operate(p0, lows0, highs0)
    wq = q0 * dinv_ref[...]
    put_halo(1, wq)
    second = halo_copies(1)
    for copy in second:
        copy.start()

    r0 = load_ref[...]
    tile = restrict_into(jnp.zeros(tile_shape, jnp.float32), q0, 0)
    sums = (sum_all(p0 * q0), sum_all(r0 * w_ref[0]), sum_all(r0 * wq), sum_all(q0 * wq))
    for i, val in enumerate(sums):
        tile = jnp.where((trow == 0) & (tlane == HALF + i), val, tile)
    tsend[1] = tile
    send_tile(1)
    total1 = wait_tile(1)

    pq0, rr, rq, qq = (total1[0:1, HALF + i : HALF + i + 1] for i in range(4))
    rz0 = rr + coarse_dot0
    alpha0 = rz0 / pq0
    c1 = jnp.where(valid, c0 - alpha0 * total1, 0.0)
    y1 = coarse(c1)
    rz1 = rr - 2.0 * alpha0 * rq + alpha0 * alpha0 * qq + sum_all(c1 * y1)
    beta = rz1 / rz0
    own1, x1, yy1, z1 = spread(y1)

    p1 = w_ref[0] - alpha0 * w_ref[1] + own1[None] + beta * p_ref[...]
    for copy in second:
        copy.wait()

    def next_halo(first_w, second_w, first_y, second_y):
        return first_w - alpha0 * second_w + second_y + beta * (first_w + first_y)

    lows1, highs1 = (
        (
            next_halo(xrecv[0, s], xrecv[1, s], x0[s][None], x1[s][None]),
            next_halo(yrecv[0, s], yrecv[1, s], yy0[s][None], yy1[s][None]),
            next_halo(zrecv[0, s], zrecv[1, s], z0[s], z1[s]),
        )
        for s in range(2)
    )
    q1 = operate(p1, lows1, highs1)
    tsend[2] = jnp.where((trow == 0) & (tlane == 0), sum_all(p1 * q1), 0.0)
    send_tile(2)
    q_ref[...] = p1
    drain_tile(0)
    drain_tile(1)
    total2 = wait_tile(2)
    alpha1 = rz1 / total2[0:1, 0:1]
    drop = alpha0 * p_ref[...] + alpha1 * q_ref[...]
    drop_ref[...] = drop
    flow_ref[...] = links[0] * (drop - pltpu.roll(drop, rows - 1, 1))
    drain_tile(2)


def run_cg(sizes, load_current, pad_cond, cond_x, cond_y, via_map):
    sx, sy, sl = sizes
    n = sx * sy * sl
    layers, rows, cols = load_current.shape
    field = (layers, rows, cols)
    f32 = jnp.float32
    vmem = pltpu.VMEM
    dma = pltpu.SemaphoreType.DMA
    spec = pl.BlockSpec(memory_space=pltpu.VMEM)
    return pl.pallas_call(
        functools.partial(cg_kernel, sizes),
        out_shape=(jax.ShapeDtypeStruct(field, f32), jax.ShapeDtypeStruct(field, f32)),
        in_specs=[spec] * 5,
        out_specs=(spec, spec),
        scratch_shapes=[
            vmem((3,) + field, f32),
            vmem((3,) + field, f32),
            vmem(field, f32),
            vmem((2,) + field, f32),
            vmem(field, f32),
            vmem(field, f32),
            vmem((2, 2, layers, 1, cols), f32),
            vmem((2, 2, layers, 1, cols), f32),
            vmem((2, 2, layers, rows, LANES), f32),
            vmem((2, 2, rows, cols), f32),
            vmem((layers, 1, cols), f32),
            vmem((layers, 1, cols), f32),
            vmem((layers, rows, LANES), f32),
            vmem((rows, cols), f32),
            vmem((3, KX * sx, LANES), f32),
            vmem((3, n - 1, KX * sx, LANES), f32),
            dma((3,)),
            dma((3,)),
            dma((2, 6)),
            dma((2, 6)),
            dma((3,)),
            dma((3,)),
        ],
        compiler_params=pltpu.CompilerParams(
            collective_id=0, has_side_effects=True, vmem_limit_bytes=48 * 1024 * 1024
        ),
    )(load_current, pad_cond, cond_x, cond_y, via_map)


def gather_kernel(flow_ref, index_ref, out_ref, hi_ref, lo_ref, acc_ref):
    layers, rows, cols = flow_ref.shape
    trees, segs = index_ref.shape
    per = segs // layers
    blocks = cols // LANES
    half = trees // 2
    index = index_ref[...]
    source = iota((segs, segs), 0)
    target = iota((segs, segs), 1)
    sort = (source == (target % per) * layers + target // per).astype(jnp.bfloat16)
    hi = jnp.dot((index // LANES).astype(jnp.bfloat16), sort, preferred_element_type=jnp.float32)
    lo = jnp.dot((index % LANES).astype(jnp.bfloat16), sort, preferred_element_type=jnp.float32)
    hi = hi.astype(jnp.int32)
    lo = lo.astype(jnp.int32)
    left = iota((half, LANES), 1) < per

    def pack(v, l):
        base = (l // 2) * LANES
        top, low = v[:half, base : base + LANES], v[half:, base : base + LANES]
        if l % 2 == 0:
            return jnp.where(left, top, pltpu.roll(low, per, 1))
        return jnp.where(left, pltpu.roll(top, per, 1), low)

    for l in range(layers):
        hi_ref[l] = pack(hi, l)
        lo_ref[l] = pack(lo, l)
    for l in range(layers):
        want = hi_ref[l]
        lane = lo_ref[l]

        acc = jnp.zeros((half, LANES), jnp.float32)
        for i in range(rows - 1):
            for b in range(blocks):
                row = flow_ref[l, i : i + 1, b * LANES : (b + 1) * LANES]
                table = jnp.broadcast_to(row, (half, LANES))
                got = jnp.take_along_axis(table, lane, axis=1, mode="promise_in_bounds")
                acc = jnp.where(want == i * blocks + b, got, acc)
        acc_ref[l] = acc
    tops, lows = [], []
    for l in range(0, layers, 2):
        even, odd = acc_ref[l], acc_ref[l + 1]
        tops.append(jnp.where(left, even, pltpu.roll(odd, per, 1)))
        lows.append(jnp.where(left, pltpu.roll(even, per, 1), odd))
    sorted_flow = jnp.concatenate(
        [jnp.concatenate(tops, axis=1), jnp.concatenate(lows, axis=1)], axis=0
    )
    back = (target == (source % per) * layers + source // per).astype(jnp.float32)
    out_ref[...] = jnp.dot(
        sorted_flow, back, preferred_element_type=jnp.float32, precision=lax.Precision.HIGHEST
    )


def gather_current(flow, branch_index):
    layers = flow.shape[0]
    trees, segs = branch_index.shape
    packed = (layers, trees // 2, LANES)
    spec = pl.BlockSpec(memory_space=pltpu.VMEM)
    return pl.pallas_call(
        gather_kernel,
        out_shape=jax.ShapeDtypeStruct((trees, segs), jnp.float32),
        in_specs=[spec, spec],
        out_specs=spec,
        scratch_shapes=[
            pltpu.VMEM(packed, jnp.int32),
            pltpu.VMEM(packed, jnp.int32),
            pltpu.VMEM(packed, jnp.float32),
        ],
    )(flow, branch_index)


def per_device(
    load_current,
    pad_cond,
    cond_x,
    cond_y,
    via_map,
    branch_index,
    tree_owner,
    initial_stress,
    block_inverse,
):
    size_x = lax.axis_size("gx")
    size_y = lax.axis_size("gy")
    size_l = lax.axis_size("layer")
    drop, field = run_cg(
        (size_x, size_y, size_l), load_current, pad_cond, cond_x, cond_y, via_map
    )
    current = gather_current(field, branch_index)
    trees_dev, segs = initial_stress.shape
    owners_count = size_x * size_y
    capacity = 2 * trees_dev // owners_count
    owners = tree_owner[:, 0]
    hits = (owners[:, None] == jnp.arange(owners_count, dtype=jnp.int32)[None, :]).astype(jnp.int32)
    slot_rank = jnp.sum((jnp.cumsum(hits, axis=0) - hits) * hits, axis=1)
    payload = jnp.stack([current, initial_stress])
    outgoing = (
        jnp.zeros((2, owners_count, capacity, segs), jnp.float32)
        .at[:, owners, slot_rank]
        .set(payload)
    )
    inverse = block_inverse[0]
    piece = lax.all_to_all(outgoing, ("gx", "gy"), split_axis=1, concat_axis=1, tiled=True)
    count = piece.shape[2]
    flow = piece[0].reshape(-1, segs)
    stress = piece[1].reshape(-1, segs)
    for step in range(STEPS):
        stress = jnp.einsum(
            "ts,us->tu", stress + KAPPA * flow, inverse, precision=lax.Precision.HIGHEST
        )
    returning = stress.reshape(owners_count, count, segs)
    solved = lax.all_to_all(returning, ("gx", "gy"), split_axis=0, concat_axis=0, tiled=True)
    final_stress = solved[owners, slot_rank]
    return (drop, final_stress)


def solution(mesh):
    return jax.shard_map(
        per_device,
        mesh=mesh,
        in_specs=(
            P("layer", "gx", "gy"),
            P("layer", "gx", "gy"),
            P("layer", "gx", "gy"),
            P("layer", "gx", "gy"),
            P("layer", "gx", "gy"),
            P(("gx", "gy", "layer"), None),
            P(("gx", "gy", "layer"), None),
            P(("gx", "gy", "layer"), None),
            P(("gx", "gy"), None, None),
        ),
        out_specs=(P("layer", "gx", "gy"), P(("gx", "gy", "layer"), None)),
        check_vma=False,
    )
```

time: 904 us -> 87.3 us (0.10)
  local copies, waits for them, and re-layouts: 553 us -> 13.4 us
  blocking collectives: 267 us -> 20 us
  starting transfers between devices: 38 us -> 3.93 us
  Pallas kernels: 0 us -> 33.8 us
  waiting for transfers between devices: 27 us -> 9.13 us
    gather x3 -> x0, local copies, waits for them, and re-layouts: 542 us -> none  [per_device(): current = flat_link[cell] * (flat_drop[cell] - flat_drop[cell + cols])]
    all_gather x3 -> x0, blocking collectives: 120 us -> none  [collect(): lax.all_gather(small.reshape(1, KX * KY), ('gx', 'gy', 'layer'), axis=0,...]
    psum x3 -> x0, blocking collectives: 116 us -> none  [total(): return lax.psum(values, ('gx', 'gy', 'layer'))]
    ppermute x17 -> x0, starting transfers between devices: 38 us -> none  [the longest x9 27.6 us: padded_2(): lax.ppermute(lax.slice_in_dim(block, block.shape[dim] - width, None, axis...]
    pallas_call x0 -> x2, Pallas kernels: none -> 33.8 us  [the longest x1 26 us: run_cg(): pl.pallas_call(functools.partial(cg_kernel, sizes), out_shape=(jax.ShapeD...]
    ppermute x17 -> x0, waiting for transfers between devices: 27 us -> none  [the longest x8 22.5 us: padded_2(): lax.ppermute(lax.slice_in_dim(block, 0, width, axis=dim), axis, backward)]
    all_to_all x1 -> x0, blocking collectives: 12.1 us -> none  [per_device(): lax.all_to_all(returning, ('gx', 'gy'), split_axis=0, concat_axis=0, tile...]
    all_to_all x0 -> x1, waiting for transfers between devices: none -> 9.13 us  [per_device(): lax.all_to_all(returning, ('gx', 'gy'), split_axis=0, concat_axis=0, tile...]
  transfers between devices with their start and end apart: 17 -> 1, of which waited for: 11 -> 1; matrix products, arithmetic and copies ran while one was open for 0% -> 0% of each run, Pallas kernels for 0% -> 0%
where the time goes in v1:
time: 87.3 us; the launch traced here: 86.9 us
  Pallas kernels  33.8 us (39%)
  blocking collectives  20 us (23%)
  local copies, waits for them, and re-layouts  13.4 us (15%)
  waiting for transfers between devices  9.13 us (10%)
  matrix products  4 us (5%)
  starting transfers between devices  3.93 us (5%)
  other arithmetic  1.92 us (2%)
    pallas_call x1, Pallas kernels, run_cg(): pl.pallas_call(functools.partial(cg_kernel, sizes), out_shape=(jax.ShapeD...  26 us
    all_to_all x1, blocking collectives, per_device(): lax.all_to_all(outgoing, ('gx', 'gy'), split_axis=1, concat_axis=1, tiled...  20 us
    all_to_all x1, waiting for transfers between devices, per_device(): lax.all_to_all(returning, ('gx', 'gy'), split_axis=0, concat_axis=0, tile...  9.13 us
    pallas_call x1, Pallas kernels, gather_current(): pl.pallas_call(gather_kernel, out_shape=jax.ShapeDtypeStruct((trees, segs...  7.78 us
    scatter x1, local copies, waits for them, and re-layouts, per_device(): outgoing = jnp.zeros((2, owners_count, capacity, segs), jnp.float32).at[:...  5.78 us
    unnamed x21, local copies, waits for them, and re-layouts  5.27 us
    dot_general x8, matrix products, per_device(): jnp.einsum('ts,us->tu', stress + KAPPA * flow, inverse, precision=lax.Pre...  4 us
    all_to_all x1, starting transfers between devices, per_device(): lax.all_to_all(returning, ('gx', 'gy'), split_axis=0, concat_axis=0, tile...  3.93 us
  transfers between devices with their start and end apart: 1, of which 1 were waited for; matrix products, arithmetic and copies ran while one was open for 0% of the time, Pallas kernels for 0%

profile of v1, /device:TPU:0, one launch (start us, length us, event | category | flops | bytes accessed | tf_op | source)
XLA Modules:
  0.0 86.9 jit_solution(8034868602396343986)
XLA Ops:
  0.7 0.7 copy-done.8
  1.8 0.4 copy-done.1
  2.3 0.9 %copy-done.3 = f32[4,16,512]{2,1,0:T(8,128)S(1)} copy-done((f32[4,16,512]{2,1,0:T(8,128)S(1)}, f32[4,16,512]{2,1,0:T(8,128)}, u32[]{:S(2)}) %copy-start.3) | copy-done | bytes 131096
  3.2 0.9 %copy-done.4 = f32[4,16,512]{2,1,0:T(8,128)S(1)} copy-done((f32[4,16,512]{2,1,0:T(8,128)S(1)}, f32[4,16,512]{2,1,0:T(8,128)}, u32[]{:S(2)}) %copy-start.4) | copy-done | bytes 131096
  4.1 0.9 %copy-done.5 = s32[4,16,512]{2,1,0:T(8,128)S(1)} copy-done((s32[4,16,512]{2,1,0:T(8,128)S(1)}, s32[4,16,512]{2,1,0:T(8,128)}, u32[]{:S(2)}) %copy-start.5) | copy-done | bytes 131096
  5.0 26.0 %shard_map.104 = (f32[4,16,512]{2,1,0:T(8,128)S(1)}, f32[4,16,512]{2,1,0:T(8,128)S(1)}) custom-call(f32[4,16,512]{2,1,0:T(8,128)S(1)} %copy-done.1, f32[4,16,512]{2,1,0:T(8,128)S(1)} %copy-done.2, f32[4,16,512]{2,1,0:T(8,128)S(1)} %copy-done.3, f32[4,16,512]{2,1,0:T(8,128)S(1)} %copy-done.4, s32[4,16,512]{2,1,0:T(8,128)S(1)} %copy-done.5), custom_call_target="tpu_custom_call" | custom-call | tf_op jit(solution)/shard_map/pallas_call | solution.py:326
  31.0 0.6 copy-done.6
  31.7 7.8 %shard_map.105 = f32[128,256]{1,0:T(8,128)} custom-call(f32[4,16,512]{2,1,0:T(8,128)} %copy-done.6, s32[128,256]{1,0:T(8,128)} %index_ref.1), custom_call_target="tpu_custom_call" | custom-call | tf_op jit(solution)/shard_map/pallas_call | solution.py:418
  39.5 0.9 %maximum_bitcast_fusion = f32[128,2,256]{2,0,1:T(8,128)S(1)} fusion(f32[1,128,256]{2,1,0:T(8,128)S(1)} %bitcast.56, f32[1,128,256]{2,1,0:T(8,128)} %bitcast.55), kind=kLoop, calls=%fused_computation.11 | loop fusion | flops 65536 | bytes 524288 | tf_op jit(solution)/shard_map/stack | solution.py:455
  40.8 5.8 %scatter_fusion = f32[2,16,16,256]{3,0,2,1:T(2,128)S(1)} fusion(f32[2,16,16,256]{3,0,2,1:T(2,128)S(1)} %broadcast_in_dim.2, s32[128]{0:T(128)S(1)} %get-tuple-element.6, f32[128,2,256]{2,1,0:T(2,128)S(1)} %copy.11), kind=kCustom, calls=%fused_computation.1 | custom fusion | bytes 787456 | tf_op jit(solution)/shard_map/scatter | solution.py:459
  46.6 20.0 %all_to_all.10 = f32[2,16,16,256]{3,0,2,1:T(2,128)S(1)} all-to-all(f32[2,16,16,256]{3,0,2,1:T(2,128)S(1)} %scatter_fusion), channel_id=1, replica_groups=mesh['gx'=4,'gy'=4,'layer'=2] {'gx','gy'}, dimensions={1} | all-to-all | bytes 1048576 | tf_op jit(solution)/shard_map/all_to_all | solution.py:462
  66.6 0.6 slice_add_fusion
  67.2 0.4 convolution_add_fusion.6
  67.6 0.4 convolution_add_fusion.5
  68.0 0.4 convolution_add_fusion.4
  68.5 0.4 convolution_add_fusion.3
  68.9 0.4 convolution_add_fusion.2
  69.3 0.4 convolution_add_fusion.1
  69.7 0.4 convolution_add_fusion
  70.1 1.1 %fusion = f32[16,16,256]{2,1,0:T(8,128)} fusion(f32[16,16,256]{2,1,0:T(8,128)S(1)} %bitcast.53, f32[1,256,256]{2,1,0:T(8,128)S(1)} %copy-done), kind=kOutput, calls=%fused_computation.12 | convolution fusion | flops 201326592 | bytes 786432 | tf_op jit(solution)/shard_map/ts,us->tu/dot_general | solution.py:467
  71.3 3.9 %all-to-all-start.1 = ((f32[16,16,256]{2,1,0:T(8,128)}), f32[16,16,256]{2,1,0:T(8,128)S(1)}, u32[]{:S(2)}, u32[]{:S(2)}) async-start(f32[16,16,256]{2,1,0:T(8,128)} %fusion), calls=%async_computation.1 | async-start | bytes 524288 | tf_op jit(solution)/shard_map/all_to_all | solution.py:471
  75.2 9.1 %all-to-all-done.1 = f32[16,16,256]{2,1,0:T(8,128)S(1)} async-done(((f32[16,16,256]{2,1,0:T(8,128)}), f32[16,16,256]{2,1,0:T(8,128)S(1)}, u32[]{:S(2)}, u32[]{:S(2)}) %all-to-all-start.1) | async-done | bytes 262176 | tf_op jit(solution)/shard_map/all_to_all | solution.py:471
  84.3 1.9 %gather_fusion = f32[128,256]{1,0:T(8,128)} fusion(f32[16,16,256]{2,1,0:T(8,128)S(1)} %all-to-all-done.1, s32[128]{0:T(128)S(1)} %bitcast.52), kind=kCustom, calls=%fused_computation | custom fusion | bytes 263168 | tf_op jit(solution)/shard_map/gather | solution.py:472
  86.3 0.7 copy.16
  (20 shorter events, 1.0 us)
Async XLA Ops:
  0.6 66.6 %copy-start = (f32[1,256,256]{2,1,0:T(8,128)S(1)}, f32[1,256,256]{2,1,0:T(8,128)}, u32[]{:S(2)}) copy-start(f32[1,256,256]{2,1,0:T(8,128)} %param.17) | copy-start | bytes 786436
  0.6 0.7 copy-start.8
  1.3 0.9 %copy-start.1 = (f32[4,16,512]{2,1,0:T(8,128)S(1)}, f32[4,16,512]{2,1,0:T(8,128)}, u32[]{:S(2)}) copy-start(f32[4,16,512]{2,1,0:T(8,128)} %load_ref.1) | copy-start | bytes 393220
  1.3 1.0 %copy-start.2 = (f32[4,16,512]{2,1,0:T(8,128)S(1)}, f32[4,16,512]{2,1,0:T(8,128)}, u32[]{:S(2)}) copy-start(f32[4,16,512]{2,1,0:T(8,128)} %pad_ref.1) | copy-start | bytes 393220
  2.3 0.9 %copy-start.3 = (f32[4,16,512]{2,1,0:T(8,128)S(1)}, f32[4,16,512]{2,1,0:T(8,128)}, u32[]{:S(2)}) copy-start(f32[4,16,512]{2,1,0:T(8,128)} %cx_ref.1) | copy-start | bytes 393220
  3.2 0.9 %copy-start.4 = (f32[4,16,512]{2,1,0:T(8,128)S(1)}, f32[4,16,512]{2,1,0:T(8,128)}, u32[]{:S(2)}) copy-start(f32[4,16,512]{2,1,0:T(8,128)} %cy_ref.1) | copy-start | bytes 393220
  4.1 0.9 %copy-start.5 = (s32[4,16,512]{2,1,0:T(8,128)S(1)}, s32[4,16,512]{2,1,0:T(8,128)}, u32[]{:S(2)}) copy-start(s32[4,16,512]{2,1,0:T(8,128)} %via_ref.1) | copy-start | bytes 393220
  31.0 0.7 copy-start.6
  31.7 7.8 %copy-start.7 = (f32[128,256]{1,0:T(8,128)S(1)}, f32[128,256]{1,0:T(8,128)}, u32[]{:S(2)}) copy-start(f32[128,256]{1,0:T(8,128)} %param.16) | copy-start | bytes 393220
  71.3 13.1 %all-to-all-start.1 = ((f32[16,16,256]{2,1,0:T(8,128)}), f32[16,16,256]{2,1,0:T(8,128)S(1)}, u32[]{:S(2)}, u32[]{:S(2)}) async-start(f32[16,16,256]{2,1,0:T(8,128)} %fusion), calls=%async_computation.1 | async-start | bytes 524288 | tf_op jit(solution)/shard_map/all_to_all | solution.py:471

commit v2 on v1

--- a/solution.py
+++ b/solution.py
@@ -34,12 +34,17 @@
 
 def cg_kernel(
     sizes,
-    load_ref, pad_ref, cx_ref, cy_ref, via_ref,
-    drop_ref, flow_ref,
+    capacity,
+    load_in, pad_in, cx_in, cy_in, via_in, index_in, stress_in, inverse_in, owner_ref,
+    drop_ref, final_ref,
+    load_ref, pad_ref, cx_ref, cy_ref, via_ref, index_ref, stress_ref, inverse_ref,
+    flow_ref, hi_ref, lo_ref, acc_ref, onehot_ref, base_ref, power_ref,
+    ssend, srecv, fsend, frecv, gsend, grecv,
     links, downs, dinv_ref, w_ref, p_ref, q_ref,
     xsend, xrecv, yrecv, zrecv, lxsend, lxrecv, lyrecv, lzrecv,
     tsend, trecv,
     link_send, link_recv, halo_send, halo_recv, tile_send, tile_recv,
+    in_sem, tree_send, tree_recv,
 ):
     sx, sy, sl = sizes
     n = sx * sy * sl
@@ -53,6 +58,16 @@
     def coords(flat):
         return (flat // (sy * sl), (flat // sl) % sy, flat % sl)
 
+    loads = [
+        pltpu.make_async_copy(src, dst, in_sem.at[i])
+        for i, (src, dst) in enumerate((
+            (via_in, via_ref), (cx_in, cx_ref), (cy_in, cy_ref), (load_in, load_ref),
+            (pad_in, pad_ref), (stress_in, stress_ref), (inverse_in, inverse_ref),
+            (index_in, index_ref),
+        ))
+    ]
+    for copy in loads:
+        copy.start()
     barrier = pltpu.get_barrier_semaphore()
 
     def greet(k, carry):
@@ -74,6 +89,62 @@
         (gx, gy, lax.rem(gl + sl - 1, sl)),
     )
 
+    np_ = sx * sy
+    q = gx * sy + gy
+    trees, segs = stress_ref.shape
+    slots = np_ * capacity
+    high = lax.Precision.HIGHEST
+
+    def exact(a, b):
+        return jnp.dot(a, b, preferred_element_type=jnp.float32, precision=high)
+
+    def rows_by(a, b):
+        return lax.dot_general(
+            a, b, (((1,), (1,)), ((), ())), preferred_element_type=jnp.float32, precision=high
+        )
+
+    owner_rel = lax.rem(owner_ref[...] - q + np_, np_)
+    hits = owner_rel == iota((trees, LANES), 1)
+    ahead = iota((trees, trees), 1) < iota((trees, trees), 0)
+    counts = jnp.dot(
+        ahead.astype(jnp.bfloat16), hits.astype(jnp.bfloat16), preferred_element_type=jnp.float32
+    )
+    rank = jnp.sum(jnp.where(hits, counts, 0.0), axis=1, keepdims=True).astype(jnp.int32)
+    slot = owner_rel * capacity + rank
+    onehot_ref[...] = (slot == iota((trees, slots), 1)).astype(jnp.float32)
+
+    def to_slots(v):
+        return lax.dot_general(
+            onehot_ref[...], v, (((0,), (0,)), ((), ())),
+            preferred_element_type=jnp.float32, precision=high,
+        ).reshape(np_, capacity, segs)
+
+    def peer(k):
+        flat = lax.rem(q + k, np_)
+        return (flat // sy, flat % sy, gl)
+
+    def exchange(phase, src, dst, sign):
+        def one(k, carry):
+            pltpu.make_async_remote_copy(
+                src_ref=src.at[k],
+                dst_ref=dst.at[k - 1],
+                send_sem=tree_send.at[phase],
+                recv_sem=tree_recv.at[phase],
+                device_id=peer(k if sign > 0 else np_ - k),
+                device_id_type=MESH,
+            ).start()
+            return carry
+
+        lax.fori_loop(1, np_, one, 0)
+
+    def arrived(phase, dst):
+        pltpu.make_async_copy(dst, dst, tree_recv.at[phase]).wait()
+
+    def sent(phase, dst):
+        pltpu.make_async_copy(dst, dst, tree_send.at[phase]).wait()
+
+    for copy in loads[:5]:
+        copy.wait()
     shape = (layers, rows, cols)
     plane_of = iota(shape, 0)
     row_of = iota(shape, 1)
@@ -173,6 +244,12 @@
         copy.start()
     send_tile(0)
 
+    for copy in loads[5:]:
+        copy.wait()
+    ssend[...] = to_slots(stress_ref[...])
+    exchange(0, ssend, srecv, 1)
+    sort_lanes(index_ref, hi_ref, lo_ref, layers)
+
     for copy in link_copies:
         copy.wait()
     down_x, _, _ = from_below(links[0], lxrecv[...], lyrecv[...], lzrecv[...])
@@ -196,6 +273,11 @@
     for copy in first:
         copy.start()
 
+    b1 = inverse_ref[0]
+    b2 = exact(b1, b1)
+    power_ref[0] = b2
+    power_ref[1] = b1 + b2
+
     total0 = wait_tile(0)
     c0 = jnp.where(valid, total0, 0.0)
     cfull = jnp.where(valid, pltpu.roll(total0, LANES - HALF, 1), 0.0) + 6.0 * COARSE_G
@@ -274,6 +356,10 @@
         tile = jnp.where((trow == 0) & (tlane == HALF + i), val, tile)
     tsend[1] = tile
     send_tile(1)
+    b2 = power_ref[0]
+    b4 = exact(b2, b2)
+    power_ref[0] = b4
+    power_ref[1] = power_ref[1] + exact(b2, power_ref[1])
     total1 = wait_tile(1)
 
     pq0, rr, rq, qq = (total1[0:1, HALF + i : HALF + i + 1] for i in range(4))
@@ -304,17 +390,46 @@
     tsend[2] = jnp.where((trow == 0) & (tlane == 0), sum_all(p1 * q1), 0.0)
     send_tile(2)
     q_ref[...] = p1
+    b4 = power_ref[0]
+    b8 = exact(b4, b4)
+    mixed = KAPPA * (power_ref[1] + exact(b4, power_ref[1]))
+    power_ref[1] = exact(mixed, segment_order(segs, layers).astype(jnp.float32))
+    arrived(0, srecv)
+    base_ref[0:capacity] = rows_by(ssend[0], b8)
+    base_ref[capacity:slots] = rows_by(srecv[...].reshape(slots - capacity, segs), b8)
     drain_tile(0)
     drain_tile(1)
+    sent(0, srecv)
     total2 = wait_tile(2)
     alpha1 = rz1 / total2[0:1, 0:1]
     drop = alpha0 * p_ref[...] + alpha1 * q_ref[...]
     drop_ref[...] = drop
     flow_ref[...] = links[0] * (drop - pltpu.roll(drop, rows - 1, 1))
+    current = pick(flow_ref, hi_ref, lo_ref, acc_ref)
+    fsend[...] = to_slots(current)
+    exchange(1, fsend, frecv, 1)
     drain_tile(2)
-
-
-def run_cg(sizes, load_current, pad_cond, cond_x, cond_y, via_map):
+    arrived(1, frecv)
+    gsend[0] = base_ref[0:capacity] + rows_by(fsend[0], power_ref[1])
+    rest = rows_by(frecv[...].reshape(slots - capacity, segs), power_ref[1])
+    rest = rest + base_ref[capacity:slots]
+    gsend[1:np_] = rest.reshape(np_ - 1, capacity, segs)
+    exchange(2, gsend, grecv, -1)
+    sent(1, frecv)
+    arrived(2, grecv)
+    back = jnp.concatenate([gsend[0], grecv[...].reshape(slots - capacity, segs)], axis=0)
+    final_ref[...] = exact(onehot_ref[...], back)
+    sent(2, grecv)
+
+
+def segment_order(segs, layers):
+    per = segs // layers
+    source = iota((segs, segs), 0)
+    target = iota((segs, segs), 1)
+    return source == (target % per) * layers + target // per
+
+
+def run_all(sizes, load_current, pad_cond, cond_x, cond_y, via_map, branch_index, tree_owner, initial_stress, block_inverse):
     sx, sy, sl = sizes
     n = sx * sy * sl
     layers, rows, cols = load_current.shape
@@ -322,13 +437,44 @@
     f32 = jnp.float32
     vmem = pltpu.VMEM
     dma = pltpu.SemaphoreType.DMA
+    i32 = jnp.int32
+    trees, segs = initial_stress.shape
+    capacity = -(-2 * trees // (sx * sy) // 8) * 8
+    slots = sx * sy * capacity
+    sent = (sx * sy, capacity, segs)
+    got = (sx * sy - 1, capacity, segs)
+    packed = (layers, trees // 2, LANES)
     spec = pl.BlockSpec(memory_space=pltpu.VMEM)
+    far = pl.BlockSpec(memory_space=pl.ANY)
     return pl.pallas_call(
-        functools.partial(cg_kernel, sizes),
-        out_shape=(jax.ShapeDtypeStruct(field, f32), jax.ShapeDtypeStruct(field, f32)),
-        in_specs=[spec] * 5,
+        functools.partial(cg_kernel, sizes, capacity),
+        out_shape=(
+            jax.ShapeDtypeStruct(field, f32), jax.ShapeDtypeStruct((trees, segs), f32)
+        ),
+        in_specs=[far] * 8 + [spec],
         out_specs=(spec, spec),
         scratch_shapes=[
+            vmem(field, f32),
+            vmem(field, f32),
+            vmem(field, f32),
+            vmem(field, f32),
+            vmem(field, i32),
+            vmem((trees, segs), i32),
+            vmem((trees, segs), f32),
+            vmem((1, segs, segs), f32),
+            vmem(field, f32),
+            vmem(packed, i32),
+            vmem(packed, i32),
+            vmem(packed, f32),
+            vmem((trees, slots), f32),
+            vmem((slots, segs), f32),
+            vmem((2, segs, segs), f32),
+            vmem(sent, f32),
+            vmem(got, f32),
+            vmem(sent, f32),
+            vmem(got, f32),
+            vmem(sent, f32),
+            vmem(got, f32),
             vmem((3,) + field, f32),
             vmem((3,) + field, f32),
             vmem(field, f32),
@@ -351,23 +497,25 @@
             dma((2, 6)),
             dma((3,)),
             dma((3,)),
+            dma((8,)),
+            dma((3,)),
+            dma((3,)),
         ],
         compiler_params=pltpu.CompilerParams(
-            collective_id=0, has_side_effects=True, vmem_limit_bytes=48 * 1024 * 1024
+            collective_id=0, has_side_effects=True, vmem_limit_bytes=56 * 1024 * 1024
         ),
-    )(load_current, pad_cond, cond_x, cond_y, via_map)
-
-
-def gather_kernel(flow_ref, index_ref, out_ref, hi_ref, lo_ref, acc_ref):
-    layers, rows, cols = flow_ref.shape
+    )(
+        load_current, pad_cond, cond_x, cond_y, via_map,
+        branch_index, initial_stress, block_inverse, tree_owner,
+    )
+
+
+def sort_lanes(index_ref, hi_ref, lo_ref, layers):
     trees, segs = index_ref.shape
     per = segs // layers
-    blocks = cols // LANES
     half = trees // 2
     index = index_ref[...]
-    source = iota((segs, segs), 0)
-    target = iota((segs, segs), 1)
-    sort = (source == (target % per) * layers + target // per).astype(jnp.bfloat16)
+    sort = segment_order(segs, layers).astype(jnp.bfloat16)
     hi = jnp.dot((index // LANES).astype(jnp.bfloat16), sort, preferred_element_type=jnp.float32)
     lo = jnp.dot((index % LANES).astype(jnp.bfloat16), sort, preferred_element_type=jnp.float32)
     hi = hi.astype(jnp.int32)
@@ -384,10 +532,16 @@
     for l in range(layers):
         hi_ref[l] = pack(hi, l)
         lo_ref[l] = pack(lo, l)
+
+
+def pick(flow_ref, hi_ref, lo_ref, acc_ref):
+    layers, rows, cols = flow_ref.shape
+    blocks = cols // LANES
+    half = hi_ref.shape[1]
+    left = iota((half, LANES), 1) < LANES // 2
     for l in range(layers):
         want = hi_ref[l]
         lane = lo_ref[l]
-
         acc = jnp.zeros((half, LANES), jnp.float32)
         for i in range(rows - 1):
             for b in range(blocks):
@@ -399,33 +553,11 @@
     tops, lows = [], []
     for l in range(0, layers, 2):
         even, odd = acc_ref[l], acc_ref[l + 1]
-        tops.append(jnp.where(left, even, pltpu.roll(odd, per, 1)))
-        lows.append(jnp.where(left, pltpu.roll(even, per, 1), odd))
-    sorted_flow = jnp.concatenate(
+        tops.append(jnp.where(left, even, pltpu.roll(odd, LANES // 2, 1)))
+        lows.append(jnp.where(left, pltpu.roll(even, LANES // 2, 1), odd))
+    return jnp.concatenate(
         [jnp.concatenate(tops, axis=1), jnp.concatenate(lows, axis=1)], axis=0
     )
-    back = (target == (source % per) * layers + source // per).astype(jnp.float32)
-    out_ref[...] = jnp.dot(
-        sorted_flow, back, preferred_element_type=jnp.float32, precision=lax.Precision.HIGHEST
-    )
-
-
-def gather_current(flow, branch_index):
-    layers = flow.shape[0]
-    trees, segs = branch_index.shape
-    packed = (layers, trees // 2, LANES)
-    spec = pl.BlockSpec(memory_space=pltpu.VMEM)
-    return pl.pallas_call(
-        gather_kernel,
-        out_shape=jax.ShapeDtypeStruct((trees, segs), jnp.float32),
-        in_specs=[spec, spec],
-        out_specs=spec,
-        scratch_shapes=[
-            pltpu.VMEM(packed, jnp.int32),
-            pltpu.VMEM(packed, jnp.int32),
-            pltpu.VMEM(packed, jnp.float32),
-        ],
-    )(flow, branch_index)
 
 
 def per_device(
@@ -442,35 +574,18 @@
     size_x = lax.axis_size("gx")
     size_y = lax.axis_size("gy")
     size_l = lax.axis_size("layer")
-    drop, field = run_cg(
-        (size_x, size_y, size_l), load_current, pad_cond, cond_x, cond_y, via_map
-    )
-    current = gather_current(field, branch_index)
-    trees_dev, segs = initial_stress.shape
-    owners_count = size_x * size_y
-    capacity = 2 * trees_dev // owners_count
-    owners = tree_owner[:, 0]
-    hits = (owners[:, None] == jnp.arange(owners_count, dtype=jnp.int32)[None, :]).astype(jnp.int32)
-    slot_rank = jnp.sum((jnp.cumsum(hits, axis=0) - hits) * hits, axis=1)
-    payload = jnp.stack([current, initial_stress])
-    outgoing = (
-        jnp.zeros((2, owners_count, capacity, segs), jnp.float32)
-        .at[:, owners, slot_rank]
-        .set(payload)
-    )
-    inverse = block_inverse[0]
-    piece = lax.all_to_all(outgoing, ("gx", "gy"), split_axis=1, concat_axis=1, tiled=True)
-    count = piece.shape[2]
-    flow = piece[0].reshape(-1, segs)
-    stress = piece[1].reshape(-1, segs)
-    for step in range(STEPS):
-        stress = jnp.einsum(
-            "ts,us->tu", stress + KAPPA * flow, inverse, precision=lax.Precision.HIGHEST
-        )
-    returning = stress.reshape(owners_count, count, segs)
-    solved = lax.all_to_all(returning, ("gx", "gy"), split_axis=0, concat_axis=0, tiled=True)
-    final_stress = solved[owners, slot_rank]
-    return (drop, final_stress)
+    return run_all(
+        (size_x, size_y, size_l),
+        load_current,
+        pad_cond,
+        cond_x,
+        cond_y,
+        via_map,
+        branch_index,
+        tree_owner,
+        initial_stress,
+        block_inverse,
+    )
 
 
 def solution(mesh):

time: 87.3 us -> 59.5 us (0.68)
  Pallas kernels: 33.8 us -> 54.9 us
  blocking collectives: 20 us -> 0 us
  local copies, waits for them, and re-layouts: 13.4 us -> 3.65 us
  waiting for transfers between devices: 9.13 us -> 0 us
  matrix products: 4 us -> 0 us
  starting transfers between devices: 3.93 us -> 0 us
  other arithmetic: 1.92 us -> 0 us
    pallas_call x2 -> x1, Pallas kernels: 33.8 us -> 54.9 us  [run_all(): pl.pallas_call(functools.partial(cg_kernel, sizes, capacity), out_shape=(...]
    all_to_all x1 -> x0, blocking collectives: 20 us -> none  [per_device(): lax.all_to_all(outgoing, ('gx', 'gy'), split_axis=1, concat_axis=1, tiled...]
    all_to_all x1 -> x0, waiting for transfers between devices: 9.13 us -> none  [per_device(): lax.all_to_all(returning, ('gx', 'gy'), split_axis=0, concat_axis=0, tile...]
    scatter x1 -> x0, local copies, waits for them, and re-layouts: 5.78 us -> none  [per_device(): outgoing = jnp.zeros((2, owners_count, capacity, segs), jnp.float32).at[:...]
    dot_general x8 -> x0, matrix products: 4 us -> none  [per_device(): jnp.einsum('ts,us->tu', stress + KAPPA * flow, inverse, precision=lax.Pre...]
    all_to_all x1 -> x0, starting transfers between devices: 3.93 us -> none  [per_device(): lax.all_to_all(returning, ('gx', 'gy'), split_axis=0, concat_axis=0, tile...]
    gather x1 -> x0, local copies, waits for them, and re-layouts: 1.93 us -> none  [per_device(): final_stress = solved[owners, slot_rank]]
    unnamed x21 -> x5, local copies, waits for them, and re-layouts: 5.27 us -> 3.65 us
  transfers between devices with their start and end apart: 1 -> 0, of which waited for: 1 -> 0; matrix products, arithmetic and copies ran while one was open for 0% -> 0% of each run, Pallas kernels for 0% -> 0%
where the time goes in v2:
time: 59.5 us; the launch traced here: 59.2 us
  Pallas kernels  54.9 us (92%)
  local copies, waits for them, and re-layouts  3.65 us (6%)
  between operations  0.65 us (1%)
    pallas_call x1, Pallas kernels, run_all(): pl.pallas_call(functools.partial(cg_kernel, sizes, capacity), out_shape=(...  54.9 us
    unnamed x5, local copies, waits for them, and re-layouts  3.65 us

profile of v2, /device:TPU:0, one launch (start us, length us, event | category | flops | bytes accessed | tf_op | source)
XLA Modules:
  0.0 59.2 jit_solution(5403361556936772465)
XLA Ops:
  0.6 1.4 %copy.11.owner_ref = s32[128,1]{1,0:T(8,128)} copy(s32[128,1]{0,1:T(1,128)} %param.15) | data formatting | bytes 1024 | tf_op args[6]
  2.0 54.9 %shard_map.104 = (f32[4,16,512]{2,1,0:T(8,128)}, f32[128,256]{1,0:T(8,128)}) custom-call(f32[4,16,512]{2,1,0:T(8,128)} %load_in.1, f32[4,16,512]{2,1,0:T(8,128)} %pad_in.1, f32[4,16,512]{2,1,0:T(8,128)} %cx_in.1, f32[4,16,512]{2,1,0:T(8,128)} %cy_in.1, s32[4,16,512]{2,1,0:T(8,128)} %via_in.1, s32[128,256]{1,0:T(8,128)} %index_in.1, f32[128,256]{1,0:T(8,128)} %stress_in.1, ...), custom_call_target="tpu_custom_call" | custom-call | tf_op jit(solution)/shard_map/pallas_call | solution.py:449
  57.0 0.0 copy-start
  57.0 1.6 %copy.14 = f32[4,16,512]{2,1,0:T(8,128)} copy(f32[4,16,512]{2,1,0:T(8,128)} %get-tuple-element.4) | data formatting | bytes 262144
  58.6 0.0 copy-done
  58.6 0.7 %copy.15 = f32[128,256]{1,0:T(8,128)} copy(f32[128,256]{1,0:T(8,128)S(1)} %copy-done) | data formatting | bytes 262144
Async XLA Ops:
  57.0 1.6 %copy-start = (f32[128,256]{1,0:T(8,128)S(1)}, f32[128,256]{1,0:T(8,128)}, u32[]{:S(2)}) copy-start(f32[128,256]{1,0:T(8,128)} %get-tuple-element.5) | copy-start | bytes 393220

commit v3 on v2

--- a/solution.py
+++ b/solution.py
@@ -38,7 +38,7 @@
     load_in, pad_in, cx_in, cy_in, via_in, index_in, stress_in, inverse_in, owner_ref,
     drop_ref, final_ref,
     load_ref, pad_ref, cx_ref, cy_ref, via_ref, index_ref, stress_ref, inverse_ref,
-    flow_ref, hi_ref, lo_ref, acc_ref, onehot_ref, base_ref, power_ref,
+    flow_ref, hi_ref, lo_ref, onehot_ref, base_ref, power_ref,
     ssend, srecv, fsend, frecv, gsend, grecv,
     links, downs, dinv_ref, w_ref, p_ref, q_ref,
     xsend, xrecv, yrecv, zrecv, lxsend, lxrecv, lyrecv, lzrecv,
@@ -51,7 +51,8 @@
     layers, rows, cols = load_ref.shape
     br, bc = rows // KX, cols // KY
     nyc = KY * sy
-    grid_rows = KX * sx
+    span = sl * KY * sy
+    grid_rows = -(-sx // 8) * 8
     gx, gy, gl = lax.axis_index("gx"), lax.axis_index("gy"), lax.axis_index("layer")
     me = (gx * sy + gy) * sl + gl
 
@@ -104,20 +105,17 @@
         )
 
     owner_rel = lax.rem(owner_ref[...] - q + np_, np_)
-    hits = owner_rel == iota((trees, LANES), 1)
-    ahead = iota((trees, trees), 1) < iota((trees, trees), 0)
+    hits = owner_rel == iota((LANES, trees), 0)
+    ahead = iota((trees, trees), 0) < iota((trees, trees), 1)
     counts = jnp.dot(
-        ahead.astype(jnp.bfloat16), hits.astype(jnp.bfloat16), preferred_element_type=jnp.float32
-    )
-    rank = jnp.sum(jnp.where(hits, counts, 0.0), axis=1, keepdims=True).astype(jnp.int32)
+        hits.astype(jnp.bfloat16), ahead.astype(jnp.bfloat16), preferred_element_type=jnp.float32
+    )
+    rank = jnp.sum(jnp.where(hits, counts, 0.0), axis=0, keepdims=True).astype(jnp.int32)
     slot = owner_rel * capacity + rank
-    onehot_ref[...] = (slot == iota((trees, slots), 1)).astype(jnp.float32)
+    onehot_ref[...] = (slot == iota((slots, trees), 0)).astype(jnp.float32)
 
     def to_slots(v):
-        return lax.dot_general(
-            onehot_ref[...], v, (((0,), (0,)), ((), ())),
-            preferred_element_type=jnp.float32, precision=high,
-        ).reshape(np_, capacity, segs)
+        return exact(onehot_ref[...], v).reshape(np_, capacity, v.shape[1])
 
     def peer(k):
         flat = lax.rem(q + k, np_)
@@ -160,22 +158,24 @@
     trow = iota(tile_shape, 0)
     tlane = iota(tile_shape, 1)
     lane0 = gl * nyc + gy * KY
-    valid = tlane < sl * nyc
+    upper = tlane >= span
+    place = lax.rem(tlane, span)
+    valid = (tlane < KX * span) & (trow < sx)
+    line = iota((1, LANES), 1)
 
     def restrict_into(tile, field, shift):
         flat = jnp.sum(field, axis=0)
         for a in range(KX):
             for b in range(KY):
                 val = sum_all(flat[a * br : (a + 1) * br, b * bc : (b + 1) * bc])
-                here = (trow == gx * KX + a) & (tlane == lane0 + b + shift)
-                tile = jnp.where(here, val, tile)
+                tile = jnp.where(line == a * span + lane0 + b + shift, val, tile)
         return tile
 
     def send_tile(phase):
         def one(k, carry):
             pltpu.make_async_remote_copy(
                 src_ref=tsend.at[phase],
-                dst_ref=trecv.at[phase, k - 1],
+                dst_ref=trecv.at[phase, pl.ds(me, 1)],
                 send_sem=tile_send.at[phase],
                 recv_sem=tile_recv.at[phase],
                 device_id=coords(lax.rem(me + k, n)),
@@ -186,15 +186,22 @@
         lax.fori_loop(1, n, one, 0)
 
     def wait_tile(phase):
-        every = trecv.at[phase]
+        every = trecv.at[phase, pl.ds(0, n - 1)]
         pltpu.make_async_copy(every, every, tile_recv.at[phase]).wait()
-        return jnp.sum(trecv[phase], axis=0) + tsend[phase]
+        group = sy * sl
+        sender = iota((group, LANES), 0)
+        total = jnp.zeros(tile_shape, jnp.float32)
+        for g in range(sx):
+            got = trecv[phase, g * group : (g + 1) * group, :]
+            got = jnp.where(sender + g * group == me, tsend[phase], got)
+            total = jnp.where(trow == g, jnp.sum(got, axis=0, keepdims=True), total)
+        return total
 
     def drain_tile(phase):
-        every = trecv.at[phase]
+        every = trecv.at[phase, pl.ds(0, n - 1)]
         pltpu.make_async_copy(every, every, tile_send.at[phase]).wait()
 
-    tile = jnp.zeros(tile_shape, jnp.float32)
+    tile = jnp.zeros((1, LANES), jnp.float32)
     tile = restrict_into(tile, load_ref[...], 0)
     tsend[0] = restrict_into(tile, pad_ref[...], HALF)
 
@@ -286,19 +293,26 @@
     def coarse(c):
         y = TAU * c / cfull
         for _ in range(SWEEPS - 1):
-            near = jnp.where(trow > 0, pltpu.roll(y, 1, 0), 0.0)
-            near += jnp.where(trow < grid_rows - 1, pltpu.roll(y, grid_rows - 1, 0), 0.0)
+            to_upper = pltpu.roll(y, span, 1)
+            to_lower = pltpu.roll(y, LANES - span, 1)
+            before = jnp.where(trow > 0, pltpu.roll(to_lower, 1, 0), 0.0)
+            after = jnp.where(trow < sx - 1, pltpu.roll(to_upper, grid_rows - 1, 0), 0.0)
+            near = jnp.where(upper, to_upper + after, to_lower + before)
             near += jnp.where(in_layer > 0, pltpu.roll(y, 1, 1), 0.0)
             near += jnp.where(in_layer < nyc - 1, pltpu.roll(y, LANES - 1, 1), 0.0)
-            near += jnp.where(tlane >= nyc, pltpu.roll(y, nyc, 1), 0.0)
-            near += jnp.where(tlane < (sl - 1) * nyc, pltpu.roll(y, LANES - nyc, 1), 0.0)
+            near += jnp.where(place >= nyc, pltpu.roll(y, nyc, 1), 0.0)
+            near += jnp.where(place < (sl - 1) * nyc, pltpu.roll(y, LANES - nyc, 1), 0.0)
             y = y + TAU * (c - (cfull * y - COARSE_G * near)) / cfull
             y = jnp.where(valid, y, 0.0)
         return y
 
     def spread(y):
-        t = pltpu.roll(y, lax.rem(grid_rows + 1 - gx * KX, grid_rows), 0)
+        t = pltpu.roll(y, lax.rem(grid_rows + 1 - gx, grid_rows), 0)
         t = pltpu.roll(t, lax.rem(LANES + 1 - lane0, LANES), 1)
+        t2 = pltpu.roll(t, LANES - span, 1)
+        order = iota(t.shape, 0)
+        at = [t2[0:1], t[1:2], t2[1:2], t[2:3]]
+        t = jnp.where(order == 0, at[0], jnp.where(order == 1, at[1], jnp.where(order == 2, at[2], at[3])))
 
         def bcast(src, r, c, height):
             return jnp.broadcast_to(src[r : r + 1, c : c + 1], (height, bc))
@@ -350,10 +364,10 @@
         copy.start()
 
     r0 = load_ref[...]
-    tile = restrict_into(jnp.zeros(tile_shape, jnp.float32), q0, 0)
+    tile = restrict_into(jnp.zeros((1, LANES), jnp.float32), q0, 0)
     sums = (sum_all(p0 * q0), sum_all(r0 * w_ref[0]), sum_all(r0 * wq), sum_all(q0 * wq))
     for i, val in enumerate(sums):
-        tile = jnp.where((trow == 0) & (tlane == HALF + i), val, tile)
+        tile = jnp.where(line == HALF + i, val, tile)
     tsend[1] = tile
     send_tile(1)
     b2 = power_ref[0]
@@ -362,7 +376,8 @@
     power_ref[1] = power_ref[1] + exact(b2, power_ref[1])
     total1 = wait_tile(1)
 
-    pq0, rr, rq, qq = (total1[0:1, HALF + i : HALF + i + 1] for i in range(4))
+    sum1 = jnp.sum(total1, axis=0, keepdims=True)
+    pq0, rr, rq, qq = (sum1[0:1, HALF + i : HALF + i + 1] for i in range(4))
     rz0 = rr + coarse_dot0
     alpha0 = rz0 / pq0
     c1 = jnp.where(valid, c0 - alpha0 * total1, 0.0)
@@ -387,7 +402,7 @@
         for s in range(2)
     )
     q1 = operate(p1, lows1, highs1)
-    tsend[2] = jnp.where((trow == 0) & (tlane == 0), sum_all(p1 * q1), 0.0)
+    tsend[2] = jnp.where(line == 0, sum_all(p1 * q1), 0.0)
     send_tile(2)
     q_ref[...] = p1
     b4 = power_ref[0]
@@ -401,25 +416,34 @@
     drain_tile(1)
     sent(0, srecv)
     total2 = wait_tile(2)
-    alpha1 = rz1 / total2[0:1, 0:1]
+    alpha1 = rz1 / jnp.sum(total2, axis=0, keepdims=True)[0:1, 0:1]
     drop = alpha0 * p_ref[...] + alpha1 * q_ref[...]
     drop_ref[...] = drop
     flow_ref[...] = links[0] * (drop - pltpu.roll(drop, rows - 1, 1))
-    current = pick(flow_ref, hi_ref, lo_ref, acc_ref)
-    fsend[...] = to_slots(current)
-    exchange(1, fsend, frecv, 1)
+    for part in range(2):
+        fsend[part] = to_slots(pick(flow_ref, hi_ref, lo_ref, part * layers // 2, layers // 2))
+        exchange(1 + part, fsend.at[part], frecv.at[part], 1)
     drain_tile(2)
-    arrived(1, frecv)
-    gsend[0] = base_ref[0:capacity] + rows_by(fsend[0], power_ref[1])
-    rest = rows_by(frecv[...].reshape(slots - capacity, segs), power_ref[1])
-    rest = rest + base_ref[capacity:slots]
+    wide = segs // 2
+    own = base_ref[0:capacity]
+    rest = base_ref[capacity:slots]
+    for part in range(2):
+        powers = power_ref[1, :, part * wide : (part + 1) * wide]
+        own = own + rows_by(fsend[part, 0], powers)
+        arrived(1 + part, frecv.at[part])
+        rest = rest + rows_by(frecv[part].reshape(slots - capacity, wide), powers)
+    gsend[0] = own
     gsend[1:np_] = rest.reshape(np_ - 1, capacity, segs)
-    exchange(2, gsend, grecv, -1)
-    sent(1, frecv)
-    arrived(2, grecv)
+    exchange(3, gsend, grecv, -1)
+    sent(1, frecv.at[0])
+    sent(2, frecv.at[1])
+    arrived(3, grecv)
     back = jnp.concatenate([gsend[0], grecv[...].reshape(slots - capacity, segs)], axis=0)
-    final_ref[...] = exact(onehot_ref[...], back)
-    sent(2, grecv)
+    final_ref[...] = lax.dot_general(
+        onehot_ref[...], back, (((0,), (0,)), ((), ())),
+        preferred_element_type=jnp.float32, precision=high,
+    )
+    sent(3, grecv)
 
 
 def segment_order(segs, layers):
@@ -465,14 +489,13 @@
             vmem(field, f32),
             vmem(packed, i32),
             vmem(packed, i32),
-            vmem(packed, f32),
-            vmem((trees, slots), f32),
+            vmem((slots, trees), f32),
             vmem((slots, segs), f32),
             vmem((2, segs, segs), f32),
             vmem(sent, f32),
             vmem(got, f32),
-            vmem(sent, f32),
-            vmem(got, f32),
+            vmem((2,) + sent[:2] + (segs // 2,), f32),
+            vmem((2,) + got[:2] + (segs // 2,), f32),
             vmem(sent, f32),
             vmem(got, f32),
             vmem((3,) + field, f32),
@@ -489,8 +512,8 @@
             vmem((layers, 1, cols), f32),
             vmem((layers, rows, LANES), f32),
             vmem((rows, cols), f32),
-            vmem((3, KX * sx, LANES), f32),
-            vmem((3, n - 1, KX * sx, LANES), f32),
+            vmem((3, 1, LANES), f32),
+            vmem((3, n, LANES), f32),
             dma((3,)),
             dma((3,)),
             dma((2, 6)),
@@ -498,15 +521,15 @@
             dma((3,)),
             dma((3,)),
             dma((8,)),
-            dma((3,)),
-            dma((3,)),
+            dma((4,)),
+            dma((4,)),
         ],
         compiler_params=pltpu.CompilerParams(
             collective_id=0, has_side_effects=True, vmem_limit_bytes=56 * 1024 * 1024
         ),
     )(
         load_current, pad_cond, cond_x, cond_y, via_map,
-        branch_index, initial_stress, block_inverse, tree_owner,
+        branch_index, initial_stress, block_inverse, tree_owner.reshape(1, trees),
     )
 
 
@@ -534,12 +557,13 @@
         lo_ref[l] = pack(lo, l)
 
 
-def pick(flow_ref, hi_ref, lo_ref, acc_ref):
+def pick(flow_ref, hi_ref, lo_ref, start, count):
     layers, rows, cols = flow_ref.shape
     blocks = cols // LANES
     half = hi_ref.shape[1]
     left = iota((half, LANES), 1) < LANES // 2
-    for l in range(layers):
+    picked = []
+    for l in range(start, start + count):
         want = hi_ref[l]
         lane = lo_ref[l]
         acc = jnp.zeros((half, LANES), jnp.float32)
@@ -549,10 +573,9 @@
                 table = jnp.broadcast_to(row, (half, LANES))
                 got = jnp.take_along_axis(table, lane, axis=1, mode="promise_in_bounds")
                 acc = jnp.where(want == i * blocks + b, got, acc)
-        acc_ref[l] = acc
+        picked.append(acc)
     tops, lows = [], []
-    for l in range(0, layers, 2):
-        even, odd = acc_ref[l], acc_ref[l + 1]
+    for even, odd in zip(picked[0::2], picked[1::2]):
         tops.append(jnp.where(left, even, pltpu.roll(odd, LANES // 2, 1)))
         lows.append(jnp.where(left, pltpu.roll(even, LANES // 2, 1), odd))
     return jnp.concatenate(

time: 59.5 us -> 52 us (0.87)
  Pallas kernels: 54.9 us -> 49 us
  local copies, waits for them, and re-layouts: 3.65 us -> 2.26 us
    pallas_call x1, Pallas kernels: 54.9 us -> 49 us  [run_all(): pl.pallas_call(functools.partial(cg_kernel, sizes, capacity), out_shape=(...]
    unnamed x5 -> x4, local copies, waits for them, and re-layouts: 3.65 us -> 2.26 us
where the time goes in v3:
time: 52 us; the launch traced here: 51.9 us
  Pallas kernels  49 us (94%)
  local copies, waits for them, and re-layouts  2.26 us (4%)
  between operations  0.65 us (1%)
    pallas_call x1, Pallas kernels, run_all(): pl.pallas_call(functools.partial(cg_kernel, sizes, capacity), out_shape=(...  49 us
    unnamed x4, local copies, waits for them, and re-layouts  2.26 us

profile of v3, /device:TPU:0, one launch (start us, length us, event | category | flops | bytes accessed | tf_op | source)
XLA Modules:
  0.0 51.9 jit_solution(15426052249605076889)
XLA Ops:
  0.6 49.0 %shard_map.104 = (f32[4,16,512]{2,1,0:T(8,128)}, f32[128,256]{1,0:T(8,128)}) custom-call(f32[4,16,512]{2,1,0:T(8,128)} %load_in.1, f32[4,16,512]{2,1,0:T(8,128)} %pad_in.1, f32[4,16,512]{2,1,0:T(8,128)} %cx_in.1, f32[4,16,512]{2,1,0:T(8,128)} %cy_in.1, s32[4,16,512]{2,1,0:T(8,128)} %via_in.1, s32[128,256]{1,0:T(8,128)} %index_in.1, f32[128,256]{1,0:T(8,128)} %stress_in.1, ...), custom_call_target="tpu_custom_call" | custom-call | tf_op jit(solution)/shard_map/pallas_call | solution.py:473
  49.6 0.0 copy-start
  49.6 1.6 %copy.13 = f32[4,16,512]{2,1,0:T(8,128)} copy(f32[4,16,512]{2,1,0:T(8,128)} %get-tuple-element.4) | data formatting | bytes 262144
  51.2 0.0 copy-done
  51.2 0.7 %copy.14 = f32[128,256]{1,0:T(8,128)} copy(f32[128,256]{1,0:T(8,128)S(1)} %copy-done) | data formatting | bytes 262144
Async XLA Ops:
  49.6 1.6 %copy-start = (f32[128,256]{1,0:T(8,128)S(1)}, f32[128,256]{1,0:T(8,128)}, u32[]{:S(2)}) copy-start(f32[128,256]{1,0:T(8,128)} %get-tuple-element.5) | copy-start | bytes 393220

commit v4 on v3

--- a/solution.py
+++ b/solution.py
@@ -56,8 +56,26 @@
     gx, gy, gl = lax.axis_index("gx"), lax.axis_index("gy"), lax.axis_index("layer")
     me = (gx * sy + gy) * sl + gl
 
-    def coords(flat):
-        return (flat // (sy * sl), (flat // sl) % sy, flat % sl)
+    ys = [lax.rem(gy + d, sy) for d in range(sy)]
+    zs = [lax.rem(gl + d, sl) for d in range(sl)]
+
+    def each_peer(act):
+        def column(dx, carry):
+            x = lax.rem(gx + dx, sx)
+            for y in ys:
+                for z in zs:
+                    act((x, y, z))
+            return carry
+
+        if sx <= 4:
+            for dx in range(1, sx):
+                column(dx, 0)
+        else:
+            lax.fori_loop(1, sx, column, 0)
+        for dy in range(sy):
+            for dz in range(sl):
+                if dy or dz:
+                    act((gx, ys[dy], zs[dz]))
 
     loads = [
         pltpu.make_async_copy(src, dst, in_sem.at[i])
@@ -71,13 +89,10 @@
         copy.start()
     barrier = pltpu.get_barrier_semaphore()
 
-    def greet(k, carry):
-        pl.semaphore_signal(
-            barrier, inc=1, device_id=coords(lax.rem(me + k, n)), device_id_type=MESH
-        )
-        return carry
-
-    lax.fori_loop(1, n, greet, 0)
+    def greet(device):
+        pl.semaphore_signal(barrier, inc=1, device_id=device, device_id_type=MESH)
+
+    each_peer(greet)
 
     up_dev = (
         (lax.rem(gx + 1, sx), gy, gl),
@@ -133,7 +148,11 @@
             ).start()
             return carry
 
-        lax.fori_loop(1, np_, one, 0)
+        if np_ <= 16:
+            for k in range(1, np_):
+                one(k, 0)
+        else:
+            lax.fori_loop(1, np_, one, 0)
 
     def arrived(phase, dst):
         pltpu.make_async_copy(dst, dst, tree_recv.at[phase]).wait()
@@ -172,18 +191,17 @@
         return tile
 
     def send_tile(phase):
-        def one(k, carry):
+        def one(device):
             pltpu.make_async_remote_copy(
                 src_ref=tsend.at[phase],
                 dst_ref=trecv.at[phase, pl.ds(me, 1)],
                 send_sem=tile_send.at[phase],
                 recv_sem=tile_recv.at[phase],
-                device_id=coords(lax.rem(me + k, n)),
+                device_id=device,
                 device_id_type=MESH,
             ).start()
-            return carry
-
-        lax.fori_loop(1, n, one, 0)
+
+        each_peer(one)
 
     def wait_tile(phase):
         every = trecv.at[phase, pl.ds(0, n - 1)]
@@ -246,16 +264,19 @@
         vz = jnp.concatenate([v[1:], z_hi[None]], axis=0)
         return vx, vy, vz
 
+    for copy in loads[5:]:
+        copy.wait()
+    ssend[...] = to_slots(stress_ref[...])
+    sort_lanes(index_ref, hi_ref, lo_ref, layers)
+    b1 = inverse_ref[0]
+    b2 = exact(b1, b1)
+    power_ref[0] = b2
+    power_ref[1] = b1 + b2
     pl.semaphore_wait(barrier, n - 1)
     for copy in link_copies:
         copy.start()
     send_tile(0)
 
-    for copy in loads[5:]:
-        copy.wait()
-    ssend[...] = to_slots(stress_ref[...])
-    exchange(0, ssend, srecv, 1)
-    sort_lanes(index_ref, hi_ref, lo_ref, layers)
 
     for copy in link_copies:
         copy.wait()
@@ -279,11 +300,8 @@
     first = halo_copies(0)
     for copy in first:
         copy.start()
-
-    b1 = inverse_ref[0]
-    b2 = exact(b1, b1)
-    power_ref[0] = b2
-    power_ref[1] = b1 + b2
+    exchange(0, ssend, srecv, 1)
+
 
     total0 = wait_tile(0)
     c0 = jnp.where(valid, total0, 0.0)

time: 52 us -> 51.3 us (0.987)
  Pallas kernels: 49 us -> 48.3 us
    pallas_call x1, Pallas kernels: 49 us -> 48.3 us  [run_all(): pl.pallas_call(functools.partial(cg_kernel, sizes, capacity), out_shape=(...]
where the time goes in v4:
time: 51.3 us; the launch traced here: 51.2 us
  Pallas kernels  48.3 us (94%)
  local copies, waits for them, and re-layouts  2.26 us (4%)
  between operations  0.65 us (1%)
    pallas_call x1, Pallas kernels, run_all(): pl.pallas_call(functools.partial(cg_kernel, sizes, capacity), out_shape=(...  48.3 us
    unnamed x4, local copies, waits for them, and re-layouts  2.26 us

profile of v4, /device:TPU:0, one launch (start us, length us, event | category | flops | bytes accessed | tf_op | source)
XLA Modules:
  0.0 51.2 jit_solution(9568235965361331884)
XLA Ops:
  0.6 48.3 %shard_map.104 = (f32[4,16,512]{2,1,0:T(8,128)}, f32[128,256]{1,0:T(8,128)}) custom-call(f32[4,16,512]{2,1,0:T(8,128)} %load_in.1, f32[4,16,512]{2,1,0:T(8,128)} %pad_in.1, f32[4,16,512]{2,1,0:T(8,128)} %cx_in.1, f32[4,16,512]{2,1,0:T(8,128)} %cy_in.1, s32[4,16,512]{2,1,0:T(8,128)} %via_in.1, s32[128,256]{1,0:T(8,128)} %index_in.1, f32[128,256]{1,0:T(8,128)} %stress_in.1, ...), custom_call_target="tpu_custom_call" | custom-call | tf_op jit(solution)/shard_map/pallas_call | solution.py:491
  48.9 0.0 copy-start
  48.9 1.6 %copy.13 = f32[4,16,512]{2,1,0:T(8,128)} copy(f32[4,16,512]{2,1,0:T(8,128)} %get-tuple-element.4) | data formatting | bytes 262144
  50.5 0.0 copy-done
  50.5 0.7 %copy.14 = f32[128,256]{1,0:T(8,128)} copy(f32[128,256]{1,0:T(8,128)S(1)} %copy-done) | data formatting | bytes 262144
Async XLA Ops:
  48.9 1.6 %copy-start = (f32[128,256]{1,0:T(8,128)S(1)}, f32[128,256]{1,0:T(8,128)}, u32[]{:S(2)}) copy-start(f32[128,256]{1,0:T(8,128)} %get-tuple-element.5) | copy-start | bytes 393220
